TPU v7x, 128 devices: a whole 4x4x4 slice. The times are simulated.
128 devices in a mesh: dom: 32 (over x, z, core), rep: 4 (over y).
Axes of the slice: x: 4, y: 4, z: 4, core: 2. Of those that a mesh axis runs over, the one named last changes fastest.
Arguments:
- features: bfloat16 [131072, 128], P(('dom', 'rep')), may hold values from -6 to 6
- adjacency: bfloat16 [131072, 1024], P(('dom', 'rep')), may hold values from -0.09375 to 0.09375
- halo_weights: bfloat16 [131072, 3072], P(('dom', 'rep')), may hold values from -0.09375 to 0.09375
- history: bfloat16 [2, 131072, 256], P(None, ('dom', 'rep')), may hold values from -6 to 6
- pull_ids: int32 [16384, 24], P(('dom', 'rep')), may hold values from 0 to 1023
- pull_count: int32 [128, 128], P(('dom', 'rep')), may hold values from 0 to 24, as said below
- w_in: bfloat16 [128, 256], replicated, may hold values from -0.5 to 0.5
- w_layers: bfloat16 [2, 256, 256], replicated, may hold values from -0.375 to 0.375
- cotangent: float32 [131072, 256], P(('dom', 'rep')), may hold values from -96 to 96
Outputs:
- final_out: bfloat16 [131072, 256], P(('dom', 'rep'))
- fresh_history: bfloat16 [2, 131072, 256], P(None, ('dom', 'rep'))
- grad_in: float32 [128, 256], replicated
- grad_layers: float32 [2, 256, 256], replicated
Inputs may be any that keep to these rules, and one draw needn't show every extreme that they name: pull_count[r, o] is 0 where o == r, and every requester r has some owner with exactly 24 live slots; slots beyond the count hold valid but unused row ids.
All inputs are finite; a program needn't handle non-finite values.
Results may differ from a plain program's by a relative error of at most 0.012.
Values may be sent and summed in bfloat16 or wider, within the bound.
A program may use at most 64 MiB of HBM per device.

v0:
```python
import math

import jax
import jax.numpy as jnp
from jax import lax
from jax.sharding import PartitionSpec as P

RESTART = 0.1
DECAY_RATE = 0.5


def silu_slope(value):
    sig = jax.nn.sigmoid(value)
    return sig * (1.0 + value * (1.0 - sig))


def local_step(node_feats, adj_block, halo_block, pulled_rows, w_in, w_layers, cot_block):
    pre_input = jnp.dot(node_feats, w_in, preferred_element_type=jnp.float32)
    initial = jax.nn.silu(pre_input).astype(jnp.bfloat16)
    current = initial
    stored = []
    refreshed = [initial]
    layers = w_layers.shape[0]
    for layer_idx in range(layers):
        mix_rate = math.log(DECAY_RATE / (layer_idx + 1) + 1.0)
        neighbour_sum = jnp.dot(adj_block, current, preferred_element_type=jnp.float32) + jnp.dot(
            halo_block, pulled_rows[layer_idx], preferred_element_type=jnp.float32
        )
        combined = (1.0 - RESTART) * neighbour_sum + RESTART * initial.astype(jnp.float32)
        combined_bf = combined.astype(jnp.bfloat16)
        pre_act = (1.0 - mix_rate) * combined + mix_rate * jnp.dot(
            combined_bf, w_layers[layer_idx], preferred_element_type=jnp.float32
        )
        stored.append((combined_bf, pre_act))
        current = jax.nn.silu(pre_act).astype(jnp.bfloat16)
        if layer_idx + 1 < layers:
            refreshed.append(current)
    grad_state = cot_block
    grad_init = jnp.zeros(cot_block.shape, jnp.float32)
    grad_list = [None] * layers
    for layer_idx in reversed(range(layers)):
        mix_rate = math.log(DECAY_RATE / (layer_idx + 1) + 1.0)
        combined_bf, pre_act = stored[layer_idx]
        grad_pre = grad_state * silu_slope(pre_act)
        grad_bf = grad_pre.astype(jnp.bfloat16)
        grad_list[layer_idx] = mix_rate * jnp.dot(
            combined_bf.T, grad_bf, preferred_element_type=jnp.float32
        )
        grad_comb = (1.0 - mix_rate) * grad_pre + mix_rate * jnp.dot(
            grad_bf, w_layers[layer_idx].T, preferred_element_type=jnp.float32
        )
        grad_init = grad_init + RESTART * grad_comb
        grad_state = (1.0 - RESTART) * jnp.dot(
            adj_block.T, grad_comb.astype(jnp.bfloat16), preferred_element_type=jnp.float32
        )
    grad_first = (grad_init + grad_state) * silu_slope(pre_input)
    grad_proj = jnp.dot(
        node_feats.T, grad_first.astype(jnp.bfloat16), preferred_element_type=jnp.float32
    )
    return (current, jnp.stack(refreshed), grad_proj, jnp.stack(grad_list))


def local(
    features, adjacency, halo_weights, history, pull_ids, pull_count, w_in, w_layers, cotangent
):
    layers = history.shape[0]
    width = history.shape[2]
    devices = lax.axis_size(("dom", "rep"))
    slots = pull_ids.shape[1]
    requests = lax.all_to_all(pull_ids, ("dom", "rep"), split_axis=0, concat_axis=0, tiled=True)
    served = history[:, requests]
    pulled = lax.all_to_all(served, ("dom", "rep"), split_axis=1, concat_axis=1, tiled=True)
    slot_idx = jnp.arange(slots, dtype=jnp.int32)[None, :]
    valid_mask = slot_idx < pull_count[0][:, None]
    pulled = jnp.where(valid_mask[None, :, :, None], pulled, jnp.zeros((), pulled.dtype)).reshape(
        layers, devices * slots, width
    )
    final_out, refreshed, grad_proj, grad_stack = local_step(
        features, adjacency, halo_weights, pulled, w_in, w_layers, cotangent
    )
    total_in, total_layers = lax.psum((grad_proj, grad_stack), ("dom", "rep"))
    factor = 1.0 / math.sqrt(features.shape[0] * devices)
    return (final_out, refreshed, total_in * factor, total_layers * factor)


def solution(mesh):
    placed = (
        P(("dom", "rep"), None),
        P(("dom", "rep"), None),
        P(("dom", "rep"), None),
        P(None, ("dom", "rep"), None),
        P(("dom", "rep"), None),
        P(("dom", "rep"), None),
        P(),
        P(),
        P(("dom", "rep"), None),
    )
    return jax.shard_map(
        local,
        mesh=mesh,
        in_specs=placed,
        out_specs=(P(("dom", "rep"), None), P(None, ("dom", "rep"), None), P(), P()),
        check_vma=False,
    )
```

profile of v0, /device:TPU:1, one launch (start us, length us, event | category | flops | bytes accessed | tf_op | source)
XLA Modules:
  0.0 320.1 jit_solution(15236201081341031791)
XLA Ops:
  7.2 0.0 copy-start
  7.2 1.0 copy.26
  8.1 21.2 %all_to_all.17 = s32[128,1,24]{2,1,0:T(1,128)S(1)} all-to-all(s32[128,1,24]{2,1,0:T(1,128)S(1)} %bitcast.74), channel_id=1, replica_groups=mesh['dom'=32,'rep'=4] {'dom','rep'}, dimensions={0} | all-to-all | bytes 24576 | tf_op jit(solution)/shard_map/all_to_all | solution.py:70
  29.3 0.1 reshape.68
  29.4 63.6 %gather_fusion = bf16[3072,2,256]{2,0,1:T(8,128)(2,1)} fusion(bf16[2,1024,256]{2,1,0:T(8,128)(2,1)} %param.12, s32[3072]{0:T(1024)S(1)} %broadcast_clamp_fusion), kind=kCustom, calls=%fused_computation | custom fusion | bytes 6303744 | tf_op jit(solution)/shard_map/gather | solution.py:71
  93.1 3.8 %copy.42 = bf16[128,24,2,256]{3,1,2,0:T(8,128)(2,1)} copy(bf16[128,24,2,256]{3,1,0,2:T(8,128)(2,1)} %bitcast.68) | data formatting | bytes 6291456 | tf_op jit(solution)/shard_map/gather | solution.py:71
  96.9 5.0 %all-to-all-start.1 = ((bf16[2,128,24,256]{3,2,0,1:T(8,128)(2,1)}), bf16[2,128,24,256]{3,2,0,1:T(8,128)(2,1)}, u32[]{:S(2)}, u32[]{:S(2)}) async-start(bf16[2,128,24,256]{3,2,0,1:T(8,128)(2,1)} %bitcast.69), calls=%async_computation.1 | async-start | bytes 6291456 | tf_op jit(solution)/shard_map/all_to_all | solution.py:72
  101.9 0.2 all-reduce.3.cloned.1.call-start
  102.1 0.0 copy-done.4
  102.1 0.1 iota_compare_fusion
  102.2 0.0 copy-done.6
  102.2 0.0 copy-done.7
  102.2 1.3 multiply_convert_fusion.2
  103.5 40.4 %all-to-all-done.1 = bf16[2,128,24,256]{3,2,0,1:T(8,128)(2,1)} async-done(((bf16[2,128,24,256]{3,2,0,1:T(8,128)(2,1)}), bf16[2,128,24,256]{3,2,0,1:T(8,128)(2,1)}, u32[]{:S(2)}, u32[]{:S(2)}) %all-to-all-start.1) | async-done | bytes 3145760 | tf_op jit(solution)/shard_map/all_to_all | solution.py:72
  143.9 2.2 broadcast_select_fusion
  146.1 0.0 slice-start
  146.1 0.2 fusion.52
  146.3 0.0 slice-start.1
  146.3 4.7 %fusion.53 = f32[256,1024]{0,1:T(8,128)S(1)} fusion(bf16[1024,3072]{1,0:T(8,128)(2,1)} %param.11, bf16[3072,256]{1,0:T(8,128)(2,1)S(1)} %bitcast.72), kind=kOutput, calls=%fused_computation.80 | convolution fusion | flops 1610612736 | bytes 8912896 | tf_op jit(solution)/shard_map/dot_general | solution.py:26
  151.1 0.0 slice-done
  151.1 0.0 slice-done.1
  151.1 1.8 fusion.54
  152.9 0.0 copy-done.1
  152.9 0.0 copy-done
  152.9 0.0 copy-start.3
  152.9 0.7 fusion.9
  153.7 0.2 copy-done.3
  153.9 0.3 fusion.3
  154.2 0.7 copy-done.2
  154.9 0.8 fusion.6
  155.8 0.0 copy-start.5
  155.8 1.3 multiply_convert_fusion
  157.1 0.0 copy-done.5
  157.1 1.3 fusion.17
  158.4 0.9 fusion.1
  159.3 0.0 copy-start.8
  159.3 1.1 fusion.14
  160.4 0.3 fusion.18
  160.7 1.3 fusion
  162.1 4.3 %fusion.19 = f32[128,256]{0,1:T(8,128)} fusion(bf16[1024,128]{1,0:T(8,128)(2,1)} %param.9, bf16[1024,1024]{1,0:T(8,128)(2,1)S(1)} %copy-done, f32[1024,256]{1,0:T(8,128)} %copy-done.8, f32[1024,256]{1,0:T(8,128)} %fusion, f32[1024,256]{1,0:T(8,128)} %get-tuple-element.21), kind=kOutput, calls=%fused_computation.32 | convolution fusion | flops 607649792 | bytes 5636096 | tf_op jit(solution)/shard_map/dot_general | solution.py:57
  166.3 1.8 pad_maximum_fusion.1
  168.1 0.0 all-reduce.3.cloned.1.call-update
  168.1 0.3 fusion.51
  168.4 2.1 pad_maximum_fusion
  170.5 139.2 %all-reduce.3.cloned.1.call-done = (f32[128,256]{0,1:T(8,128)}, f32[2,256,256]{2,1,0:T(8,128)}) async-done(((f32[128,256]{0,1:T(8,128)}, f32[2,256,256]{2,1,0:T(8,128)}), (f32[128,256]{0,1:T(8,128)}, f32[2,256,256]{2,1,0:T(8,128)})) %all-reduce.3.cloned.1.call-update) | async-done | bytes 655376 | tf_op jit(solution)/shard_map/psum | solution.py:81
  309.7 0.9 broadcast_multiply_fusion.1
  310.6 0.8 copy.34
  311.4 1.9 broadcast_multiply_fusion
  (9 shorter events, 0.0 us)
Async XLA Ops:
  7.2 145.8 %copy-start = (bf16[1024,1024]{1,0:T(8,128)(2,1)S(1)}, bf16[1024,1024]{1,0:T(8,128)(2,1)}, u32[]{:S(2)}) copy-start(bf16[1024,1024]{1,0:T(8,128)(2,1)} %param.10) | copy-start | bytes 6291460
  96.9 5.2 %copy-start.4 = (s32[1,128]{1,0:T(1,128)S(1)}, s32[1,128]{1,0:T(1,128)}, u32[]{:S(2)}) copy-start(s32[1,128]{1,0:T(1,128)} %param.14) | copy-start | bytes 1540
  96.9 5.3 %copy-start.6 = (bf16[1024,128]{1,0:T(8,128)(2,1)S(1)}, bf16[1024,128]{1,0:T(8,128)(2,1)}, u32[]{:S(2)}) copy-start(bf16[1024,128]{1,0:T(8,128)(2,1)} %param.9) | copy-start | bytes 786436
  96.9 5.3 %copy-start.7 = (bf16[128,256]{1,0:T(8,128)(2,1)S(1)}, bf16[128,256]{1,0:T(8,128)(2,1)}, u32[]{:S(2)}) copy-start(bf16[128,256]{1,0:T(8,128)(2,1)} %param.15) | copy-start | bytes 196612
  96.9 47.0 %all-to-all-start.1 = ((bf16[2,128,24,256]{3,2,0,1:T(8,128)(2,1)}), bf16[2,128,24,256]{3,2,0,1:T(8,128)(2,1)}, u32[]{:S(2)}, u32[]{:S(2)}) async-start(bf16[2,128,24,256]{3,2,0,1:T(8,128)(2,1)} %bitcast.69), calls=%async_computation.1 | async-start | bytes 6291456 | tf_op jit(solution)/shard_map/all_to_all | solution.py:72
  101.9 207.8 %all-reduce.3.cloned.1.call-start = ((), (), s32[]{:S(2)}) async-start(), calls=%async_computation.2 | async-start | bytes 1310720 | tf_op jit(solution)/shard_map/psum | solution.py:81
  103.5 49.4 %copy-start.1 = (bf16[1024,256]{1,0:T(8,128)(2,1)}, bf16[1024,256]{1,0:T(8,128)(2,1)S(1)}, u32[]{:S(2)}) copy-start(bf16[1024,256]{1,0:T(8,128)(2,1)S(1)} %get-tuple-element.20) | copy-start | bytes 1572868
  146.1 5.0 %slice-start = ((s8[6291456]{0:T(1024)(128)(4,1)}), s8[2097152]{0:T(1024)(128)(4,1)S(1)}, s32[]{:S(2)}) async-start(s8[6291456]{0:T(1024)(128)(4,1)} %bitcast.76), calls=%async_computation.3 | async-start | bytes 4194304
  146.3 4.8 %slice-start.1 = ((s8[6291456]{0:T(1024)(128)(4,1)}), s8[4194304]{0:T(1024)(128)(4,1)S(1)}, s32[]{:S(2)}) async-start(s8[6291456]{0:T(1024)(128)(4,1)} %bitcast.76), calls=%async_computation.4 | async-start | bytes 8388608
  152.9 1.0 copy-start.3
  153.9 1.0 copy-start.2
  155.8 1.3 copy-start.5
  159.3 1.1 copy-start.8
Sparse Core Ops, SparseCore 0:
  168.3 141.3 all-reduce.2
where the time goes:
time: 321 us; the launch traced here: 320 us
  waiting for transfers between devices  180 us (56%)
  local copies, waits for them, and re-layouts  70.4 us (22%)
  blocking collectives  21.2 us (7%)
  matrix products  20.2 us (6%)
  between operations  14.3 us (4%)
  other arithmetic  9.23 us (3%)
  starting transfers between devices  5.19 us (2%)
    psum x1, waiting for transfers between devices, local(): total_in, total_layers = lax.psum((grad_proj, grad_stack), ('dom', 'rep'))  139 us
    gather x2, local copies, waits for them, and re-layouts, local(): served = history[:, requests]  67.4 us
    all_to_all x1, waiting for transfers between devices, local(): lax.all_to_all(served, ('dom', 'rep'), split_axis=1, concat_axis=1, tiled...  40.4 us
    all_to_all x1, blocking collectives, local(): lax.all_to_all(pull_ids, ('dom', 'rep'), split_axis=0, concat_axis=0, til...  21.2 us
    dot_general x2, matrix products, local_step(): jnp.dot(halo_block, pulled_rows[layer_idx], preferred_element_type=jnp.fl...  6.53 us
  transfers between devices with their start and end apart: 2, of which 2 were waited for; matrix products, arithmetic and copies ran while one was open for 1% of the time, Pallas kernels for 0%

commit v1 on v0

v1 whole, which is shorter than its diff:
```python
import functools
import math
import random

import jax
import jax.numpy as jnp
from jax import lax
from jax.experimental import pallas as pl
from jax.experimental.pallas import tpu as pltpu
from jax.sharding import PartitionSpec as P

RESTART = 0.1
DECAY_RATE = 0.5
MESH = pl.DeviceIdType.MESH
BF = jnp.bfloat16
F32 = jnp.float32

ROWS = 1024
WIDTH = 256
FIN = 128
SLOTS = 24
DEVICES = 128
HALO = DEVICES * SLOTS
TILE = 256
GROUP = 16
UNITS = 32

ORDER = [(k // 32, k % 4, (k // 8) % 4, (k // 4) % 2) for k in range(1, DEVICES)]
random.Random(4).shuffle(ORDER)
MIX = [math.log(DECAY_RATE / (layer + 1) + 1.0) for layer in range(2)]


def mm(a, b):
    return jnp.dot(a, b, preferred_element_type=F32)


def slope(value, sig):
    return sig * (1.0 + value * (1.0 - sig))


def kernel(
    feat_h, adj_h, halo_h, hist_h, ids_h, cnt_h, win_h, wl_h, cot_h,
    final_h, fresh_h, gsum,
    feat, adj, halo, hist, ids, cnt, win, wl, cot,
    idsend, idrecv, idcol, send, recv, pulled,
    init, x1, fin, adj_t, feat_t, wl_t, cb0_t,
    slope_in, slope0, base, ginit, gcb, gl, grad, rsbuf, unit,
    in_sem, out_sem, id_send, id_recv, row_send, row_recv, rs_send, rs_recv, ag_send, ag_recv,
):
    dom, y = lax.axis_index("dom"), lax.axis_index("rep")
    x, z, core = dom // 8, (dom // 2) % 4, dom % 2
    me = dom * 4 + y
    fwd_x = [(x + d) % 4 * 8 for d in range(4)]
    fwd_z = [(z + d) % 4 * 2 for d in range(4)]
    fwd_y = [(y + d) % 4 for d in range(4)]
    cores = [core, 1 - core]

    def ahead(off):
        return (fwd_x[off[0]] + fwd_z[off[2]] + cores[off[3]], fwd_y[off[1]])

    def behind(off):
        return (
            fwd_x[(4 - off[0]) % 4] + fwd_z[(4 - off[2]) % 4] + cores[off[3]],
            fwd_y[(4 - off[1]) % 4],
        )

    idrecv[pl.ds(DEVICES - 1, 1), :] = jnp.full((1, DEVICES), -1, jnp.int32)
    barrier = pltpu.get_barrier_semaphore()
    for off in ORDER:
        pl.semaphore_signal(barrier, inc=1, device_id=ahead(off), device_id_type=MESH)

    loads = [
        pltpu.make_async_copy(src, dst, in_sem.at[i])
        for i, (src, dst) in enumerate(
            [
                (ids_h, ids), (cnt_h, cnt), (hist_h, hist), (feat_h, feat), (win_h, win),
                (wl_h, wl), (adj_h, adj), (halo_h, halo), (cot_h, cot),
            ]
        )
    ]
    for load in loads:
        load.start()

    loads[0].wait()
    loads[1].wait()
    slot = lax.broadcasted_iota(jnp.int32, (SLOTS, DEVICES), 0)
    wanted = jnp.where(slot < cnt[...], ids[...], -1)
    wanted = jnp.concatenate([wanted, jnp.full((DEVICES - SLOTS, DEVICES), -1, jnp.int32)], axis=0)
    idsend[...] = wanted.T

    pl.semaphore_wait(barrier, DEVICES - 1)
    for p, off in enumerate(ORDER):
        to = behind(off)
        pltpu.make_async_remote_copy(
            src_ref=idsend.at[pl.ds(to[0] * 4 + to[1], 1)], dst_ref=idrecv.at[pl.ds(p, 1)],
            send_sem=id_send, recv_sem=id_recv, device_id=to, device_id_type=MESH,
        ).start()
    recv[0, me] = jnp.zeros((2 * SLOTS, 128), BF)
    recv[1, me] = jnp.zeros((2 * SLOTS, 128), BF)
    loads[2].wait()
    ids_all = pltpu.make_async_copy(
        idrecv.at[pl.ds(0, DEVICES - 1)], idrecv.at[pl.ds(0, DEVICES - 1)], id_recv
    )
    ids_all.wait()

    idcol[...] = idrecv[...].T

    def row_copy(layer, p):
        return pltpu.make_async_remote_copy(
            src_ref=send.at[layer, p], dst_ref=recv.at[layer, me],
            send_sem=row_send.at[layer], recv_sem=row_recv.at[layer],
            device_id=ahead(ORDER[p]), device_id_type=MESH,
        )

    row_id = lax.broadcasted_iota(jnp.int32, (SLOTS, ROWS), 1)
    for first in range(0, DEVICES - 1, GROUP):
        part = range(first, min(first + GROUP, DEVICES - 1))
        one_hot = jnp.concatenate(
            [
                jnp.where(idcol[pl.ds(0, SLOTS), pl.ds(p, 1)] == row_id, 1.0, 0.0).astype(BF)
                for p in part
            ],
            axis=0,
        )
        for layer in range(2):
            rows = mm(one_hot, hist[layer]).astype(BF)
            for i, p in enumerate(part):
                mine = rows[i * SLOTS : (i + 1) * SLOTS]
                send[layer, p] = jnp.concatenate([mine[:, :128], mine[:, 128:]], axis=0)
            if layer == 0:
                for p in part:
                    row_copy(0, p).start()
    for p in range(DEVICES - 1):
        row_copy(1, p).start()

    for load in loads[3:7]:
        load.wait()
    for layer in range(2):
        wl_t[layer] = wl[layer].T
    feat_t[...] = feat[...].T

    @pl.loop(0, ROWS // TILE)
    def _(t):
        here = pl.ds(pl.multiple_of(t * TILE, TILE), TILE)
        pre = mm(feat[here, :], win[...])
        sig = jax.nn.sigmoid(pre)
        init[here, :] = (pre * sig).astype(BF)
        slope_in[here, :] = slope(pre, sig)
        adj_t[:, here] = adj[here, :].T

    fresh0 = pltpu.make_async_copy(init, fresh_h.at[0], out_sem.at[0])
    fresh0.start()

    def neighbours(state):
        @pl.loop(0, ROWS // TILE)
        def _(t):
            here = pl.ds(pl.multiple_of(t * TILE, TILE), TILE)
            base[here, :] = (1.0 - RESTART) * mm(adj[here, :], state[...]) + RESTART * init[
                here, :
            ].astype(F32)

    def unpack(layer):
        @pl.loop(0, DEVICES // 2)
        def _(o):
            both = [recv[layer, 2 * o], recv[layer, 2 * o + 1]]
            both = [jnp.concatenate([b[:SLOTS], b[SLOTS:]], axis=1) for b in both]
            rows = pl.ds(pl.multiple_of(o * 2 * SLOTS, 2 * SLOTS), 2 * SLOTS)
            pulled[rows, :] = jnp.concatenate(both, axis=0)

    def row_wait(layer):
        got = recv.at[layer, pl.ds(0, DEVICES - 1)]
        pltpu.make_async_copy(got, got, row_recv.at[layer]).wait()

    neighbours(init)
    loads[7].wait()
    loads[8].wait()
    row_wait(0)
    unpack(0)

    @pl.loop(0, ROWS // TILE)
    def _(t):
        here = pl.ds(pl.multiple_of(t * TILE, TILE), TILE)
        comb = base[here, :] + (1.0 - RESTART) * mm(halo[here, :], pulled[...])
        comb_bf = comb.astype(BF)
        cb0_t[:, here] = comb_bf.T
        pre = (1.0 - MIX[0]) * comb + MIX[0] * mm(comb_bf, wl[0])
        sig = jax.nn.sigmoid(pre)
        x1[here, :] = (pre * sig).astype(BF)
        slope0[here, :] = slope(pre, sig)

    fresh1 = pltpu.make_async_copy(x1, fresh_h.at[1], out_sem.at[1])
    fresh1.start()
    neighbours(x1)
    row_wait(1)
    unpack(1)

    gl[...] = jnp.zeros_like(gl)

    @pl.loop(0, ROWS // TILE)
    def _(t):
        here = pl.ds(pl.multiple_of(t * TILE, TILE), TILE)
        comb = base[here, :] + (1.0 - RESTART) * mm(halo[here, :], pulled[...])
        comb_bf = comb.astype(BF)
        pre = (1.0 - MIX[1]) * comb + MIX[1] * mm(comb_bf, wl[1])
        sig = jax.nn.sigmoid(pre)
        fin[here, :] = (pre * sig).astype(BF)
        g_pre = cot[here, :] * slope(pre, sig)
        e = g_pre.astype(BF)
        gl[...] += mm(comb_bf.T, e)
        g_comb = (1.0 - MIX[1]) * g_pre + MIX[1] * mm(e, wl_t[1])
        ginit[here, :] = RESTART * g_comb
        gcb[0, here, :] = g_comb.astype(BF)

    final = pltpu.make_async_copy(fin, final_h, out_sem.at[2])
    final.start()

    def owner(part, u):
        if part < 2:
            return (u, (u // 8 + (u // 2) % 4 + part) % 4)
        return (2 * u, (u // 4 + u % 4 + 2) % 4)

    def place(part, u):
        blocks = 16 if part < 2 else 8
        start = WIDTH * part + (u % blocks) * 16
        return pl.ds(pl.multiple_of(start, 16), 16), pl.ds(pl.multiple_of(u // blocks * 128, 128), 128)

    def scatter(part):
        count = UNITS if part < 2 else UNITS // 2

        @pl.loop(0, count)
        def _(i):
            u = (i + dom + 8 * y) % count
            to = owner(part, u)
            rows, lanes = place(part, u)
            own = (to[0] == dom) & (to[1] == y)

            @pl.when(own)
            def _():
                rsbuf[me] = grad[rows, lanes]

            @pl.when(jnp.logical_not(own))
            def _():
                pltpu.make_async_remote_copy(
                    src_ref=grad.at[rows, lanes], dst_ref=rsbuf.at[me],
                    send_sem=rs_send, recv_sem=rs_recv, device_id=to, device_id_type=MESH,
                ).start()

    grad[pl.ds(0, WIDTH), :] = (MIX[1] * gl[...]).astype(BF)
    scatter(0)
    gl[...] = jnp.zeros_like(gl)

    @pl.loop(0, ROWS // TILE)
    def _(t):
        here = pl.ds(pl.multiple_of(t * TILE, TILE), TILE)
        g_state = (1.0 - RESTART) * mm(adj_t[here, :], gcb[0])
        g_pre = g_state * slope0[here, :]
        e = g_pre.astype(BF)
        gl[...] += mm(cb0_t[:, here], e)
        g_comb = (1.0 - MIX[0]) * g_pre + MIX[0] * mm(e, wl_t[0])
        ginit[here, :] += RESTART * g_comb
        gcb[1, here, :] = g_comb.astype(BF)

    grad[pl.ds(WIDTH, WIDTH), :] = (MIX[0] * gl[...]).astype(BF)
    scatter(1)
    gl[pl.ds(0, FIN), :] = jnp.zeros((FIN, WIDTH), F32)

    @pl.loop(0, ROWS // TILE)
    def _(t):
        here = pl.ds(pl.multiple_of(t * TILE, TILE), TILE)
        g_state = (1.0 - RESTART) * mm(adj_t[here, :], gcb[1])
        g_first = (ginit[here, :] + g_state) * slope_in[here, :]
        gl[pl.ds(0, FIN), :] += mm(feat_t[:, here], g_first.astype(BF))

    grad[pl.ds(2 * WIDTH, FIN), :] = gl[pl.ds(0, FIN), :].astype(BF)
    scatter(2)

    turn = (y - x - z + 8) % 4
    has_unit = (turn < 2) | ((turn == 2) & (core == 0))

    @pl.when(has_unit)
    def _():
        got = rsbuf.at[pl.ds(0, DEVICES - 1)]
        pltpu.make_async_copy(got, got, rs_recv).wait()
        unit[...] = jnp.sum(rsbuf[...].astype(F32), axis=0).astype(BF)
        blocks = jnp.where(turn < 2, 16, 8)
        u = jnp.where(turn < 2, dom, dom // 2)
        rows = pl.ds(pl.multiple_of(WIDTH * turn + (u % blocks) * 16, 16), 16)
        lanes = pl.ds(pl.multiple_of(u // blocks * 128, 128), 128)
        gsum[rows, lanes] = unit[...]
        for off in ORDER:
            pltpu.make_async_remote_copy(
                src_ref=unit, dst_ref=gsum.at[rows, lanes],
                send_sem=ag_send, recv_sem=ag_recv, device_id=ahead(off), device_id_type=MESH,
            ).start()

    def drain(ref, sem):
        pltpu.make_async_copy(ref, ref, sem).wait()

    @pl.when(jnp.logical_not(has_unit))
    def _():
        drain(rsbuf.at[pl.ds(0, 80)], rs_send)
        drain(rsbuf.at[pl.ds(0, 80)], ag_recv)

    @pl.when(has_unit)
    def _():
        drain(rsbuf.at[pl.ds(0, 79)], rs_send)
        drain(rsbuf.at[pl.ds(0, 79)], ag_recv)
        drain(rsbuf.at[pl.ds(0, DEVICES - 1)], ag_send)

    drain(idsend.at[pl.ds(0, DEVICES - 1)], id_send)
    drain(send.at[0, pl.ds(0, DEVICES - 1)], row_send.at[0])
    drain(send.at[1, pl.ds(0, DEVICES - 1)], row_send.at[1])
    fresh0.wait()
    fresh1.wait()
    final.wait()


def local(
    features, adjacency, halo_weights, history, pull_ids, pull_count, w_in, w_layers, cotangent
):
    hbm = pl.BlockSpec(memory_space=pl.ANY)
    vmem = pltpu.VMEM
    dma = pltpu.SemaphoreType.DMA
    final_out, fresh, gsum = pl.pallas_call(
        kernel,
        out_shape=(
            jax.ShapeDtypeStruct((ROWS, WIDTH), BF),
            jax.ShapeDtypeStruct((2, ROWS, WIDTH), BF),
            jax.ShapeDtypeStruct((2 * WIDTH + FIN, WIDTH), BF),
        ),
        in_specs=[hbm] * 9,
        out_specs=(hbm, hbm, pl.BlockSpec(memory_space=vmem)),
        scratch_shapes=[
            vmem((ROWS, FIN), BF),
            vmem((ROWS, ROWS), BF),
            vmem((ROWS, HALO), BF),
            vmem((2, ROWS, WIDTH), BF),
            vmem((SLOTS, DEVICES), jnp.int32),
            vmem((1, DEVICES), jnp.int32),
            vmem((FIN, WIDTH), BF),
            vmem((2, WIDTH, WIDTH), BF),
            vmem((ROWS, WIDTH), F32),
            vmem((DEVICES, 128), jnp.int32),
            vmem((DEVICES, 128), jnp.int32),
            vmem((128, DEVICES), jnp.int32),
            vmem((2, DEVICES, 2 * SLOTS, 128), BF),
            vmem((2, DEVICES, 2 * SLOTS, 128), BF),
            vmem((HALO, WIDTH), BF),
            vmem((ROWS, WIDTH), BF),
            vmem((ROWS, WIDTH), BF),
            vmem((ROWS, WIDTH), BF),
            vmem((ROWS, ROWS), BF),
            vmem((FIN, ROWS), BF),
            vmem((2, WIDTH, WIDTH), BF),
            vmem((WIDTH, ROWS), BF),
            vmem((ROWS, WIDTH), F32),
            vmem((ROWS, WIDTH), F32),
            vmem((ROWS, WIDTH), F32),
            vmem((ROWS, WIDTH), F32),
            vmem((2, ROWS, WIDTH), BF),
            vmem((WIDTH, WIDTH), F32),
            vmem((2 * WIDTH + FIN, WIDTH), BF),
            vmem((DEVICES, 16, 128), BF),
            vmem((16, 128), BF),
            dma((9,)),
            dma((3,)),
            dma(()),
            dma(()),
            dma((2,)),
            dma((2,)),
            dma(()),
            dma(()),
            dma(()),
            dma(()),
        ],
        compiler_params=pltpu.CompilerParams(
            collective_id=0, has_side_effects=True, vmem_limit_bytes=48 * 2**20
        ),
    )(
        features, adjacency, halo_weights, history, pull_ids.T, pull_count, w_in, w_layers, cotangent
    )
    factor = 1.0 / math.sqrt(ROWS * DEVICES)
    sums = gsum.astype(F32) * factor
    layers = jnp.stack([sums[WIDTH : 2 * WIDTH], sums[:WIDTH]])
    return (final_out, fresh, sums[2 * WIDTH :], layers)


def solution(mesh):
    rows = P(("dom", "rep"), None)
    history = P(None, ("dom", "rep"), None)
    return jax.shard_map(
        local,
        mesh=mesh,
        in_specs=(rows, rows, rows, history, rows, rows, P(), P(), rows),
        out_specs=(rows, history, P(), P()),
        check_vma=False,
    )
```

time: 321 us -> 94 us (0.29)
  waiting for transfers between devices: 180 us -> 0 us
  Pallas kernels: 0 us -> 83.1 us
  local copies, waits for them, and re-layouts: 70.4 us -> 9 us
  blocking collectives: 21.2 us -> 0 us
  matrix products: 20.2 us -> 0 us
  between operations: 14.3 us -> 0.67 us
  other arithmetic: 9.23 us -> 0.89 us
  starting transfers between devices: 5.19 us -> 0 us
    psum x1 -> x0, waiting for transfers between devices: 139 us -> none  [local(): total_in, total_layers = lax.psum((grad_proj, grad_stack), ('dom', 'rep'))]
    pallas_call x0 -> x1, Pallas kernels: none -> 83.1 us  [local(): pl.pallas_call(kernel, out_shape=(jax.ShapeDtypeStruct((ROWS, WIDTH), BF)...]
    gather x2 -> x0, local copies, waits for them, and re-layouts: 67.4 us -> none  [local(): served = history[:, requests]]
    all_to_all x1 -> x0, waiting for transfers between devices: 40.4 us -> none  [local(): lax.all_to_all(served, ('dom', 'rep'), split_axis=1, concat_axis=1, tiled...]
    all_to_all x1 -> x0, blocking collectives: 21.2 us -> none  [local(): lax.all_to_all(pull_ids, ('dom', 'rep'), split_axis=0, concat_axis=0, til...]
    dot_general x13 -> x0, matrix products: 20.2 us -> none  [the longest x2 6.53 us: local_step(): jnp.dot(halo_block, pulled_rows[layer_idx], preferred_element_type=jnp.fl...]
    unnamed x24 -> x16, local copies, waits for them, and re-layouts: 2.69 us -> 8.3 us
    all_to_all x1 -> x0, starting transfers between devices: 4.97 us -> none  [local(): lax.all_to_all(served, ('dom', 'rep'), split_axis=1, concat_axis=1, tiled...]
  transfers between devices with their start and end apart: 2 -> 0, of which waited for: 2 -> 0; matrix products, arithmetic and copies ran while one was open for 1% -> 0% of each run, Pallas kernels for 0% -> 0%
where the time goes in v1:
time: 94 us; the launch traced here: 93.7 us
  Pallas kernels  83.1 us (88%)
  local copies, waits for them, and re-layouts  9 us (10%)
    pallas_call x1, Pallas kernels, local(): pl.pallas_call(kernel, out_shape=(jax.ShapeDtypeStruct((ROWS, WIDTH), BF)...  83.1 us
    unnamed x16, local copies, waits for them, and re-layouts  8.3 us

profile of v1, /device:TPU:1, one launch (start us, length us, event | category | flops | bytes accessed | tf_op | source)
XLA Modules:
  0.0 93.7 jit_solution(7106865320715610234)
XLA Ops:
  0.6 0.0 copy-start
  0.6 1.2 %copy-done = bf16[2,1024,256]{2,1,0:T(8,128)(2,1)S(1)} copy-done((bf16[2,1024,256]{2,1,0:T(8,128)(2,1)S(1)}, bf16[2,1024,256]{2,1,0:T(8,128)(2,1)}, u32[]{:S(2)}) %copy-start) | copy-done | bytes 1048600
  1.9 0.0 copy-start.1
  1.9 1.2 %copy-done.1 = f32[1024,256]{1,0:T(8,128)S(1)} copy-done((f32[1024,256]{1,0:T(8,128)S(1)}, f32[1024,256]{1,0:T(8,128)}, u32[]{:S(2)}) %copy-start.1) | copy-done | bytes 1048600
  3.1 0.0 copy-start.2
  3.1 0.9 %copy-done.2 = bf16[1024,128]{1,0:T(8,128)(2,1)S(1)} copy-done((bf16[1024,128]{1,0:T(8,128)(2,1)S(1)}, bf16[1024,128]{1,0:T(8,128)(2,1)}, u32[]{:S(2)}) %copy-start.2) | copy-done | bytes 262168
  4.0 0.0 copy-start.3
  4.0 0.9 %copy-done.3 = bf16[2,256,256]{2,1,0:T(8,128)(2,1)S(1)} copy-done((bf16[2,256,256]{2,1,0:T(8,128)(2,1)S(1)}, bf16[2,256,256]{2,1,0:T(8,128)(2,1)}, u32[]{:S(2)}) %copy-start.3) | copy-done | bytes 262168
  5.0 0.0 copy-start.4
  5.0 0.8 copy-done.4
  5.8 0.0 copy-start.5
  5.8 0.7 copy-done.5
  6.5 0.0 copy-start.6
  6.5 0.7 copy-done.6
  7.2 83.1 %shard_map.120 = (bf16[1024,256]{1,0:T(8,128)(2,1)S(1)}, bf16[2,1024,256]{2,1,0:T(8,128)(2,1)S(1)}, bf16[640,256]{1,0:T(8,128)(2,1)S(1)}) custom-call(bf16[1024,128]{1,0:T(8,128)(2,1)S(1)} %copy-done.2, bf16[1024,1024]{1,0:T(8,128)(2,1)} %adj_h.1, bf16[1024,3072]{1,0:T(8,128)(2,1)} %halo_h.1, bf16[2,1024,256]{2,1,0:T(8,128)(2,1)S(1)} %copy-done, ...), custom_call_target="tpu_custom_call" | custom-call | tf_op jit(solution)/shard_map/pallas_call | solution.py:324
  90.3 0.1 convert_multiply_fusion
  90.4 0.7 slice.12
  91.1 0.8 pad_maximum_fusion
  91.9 0.8 copy.15
  92.7 1.0 %copy.16 = bf16[2,1024,256]{2,1,0:T(8,128)(2,1)} copy(bf16[2,1024,256]{2,1,0:T(8,128)(2,1)S(1)} %get-tuple-element.17) | data formatting | bytes 2097152
  (1 shorter events, 0.0 us)
Async XLA Ops:
  0.6 1.2 %copy-start = (bf16[2,1024,256]{2,1,0:T(8,128)(2,1)S(1)}, bf16[2,1024,256]{2,1,0:T(8,128)(2,1)}, u32[]{:S(2)}) copy-start(bf16[2,1024,256]{2,1,0:T(8,128)(2,1)} %hist_h.1) | copy-start | bytes 3145732
  1.9 1.2 %copy-start.1 = (f32[1024,256]{1,0:T(8,128)S(1)}, f32[1024,256]{1,0:T(8,128)}, u32[]{:S(2)}) copy-start(f32[1024,256]{1,0:T(8,128)} %cot_h.1) | copy-start | bytes 3145732
  3.1 0.9 %copy-start.2 = (bf16[1024,128]{1,0:T(8,128)(2,1)S(1)}, bf16[1024,128]{1,0:T(8,128)(2,1)}, u32[]{:S(2)}) copy-start(bf16[1024,128]{1,0:T(8,128)(2,1)} %feat_h.1) | copy-start | bytes 786436
  4.0 0.9 %copy-start.3 = (bf16[2,256,256]{2,1,0:T(8,128)(2,1)S(1)}, bf16[2,256,256]{2,1,0:T(8,128)(2,1)}, u32[]{:S(2)}) copy-start(bf16[2,256,256]{2,1,0:T(8,128)(2,1)} %wl_h.1) | copy-start | bytes 786436
  5.0 0.8 copy-start.4
  5.8 0.7 copy-start.5
  6.5 0.7 copy-start.6

commit v2 on v1

v2 whole, which is shorter than its diff:
```python
import functools
import math
import random

import jax
import jax.numpy as jnp
from jax import lax
from jax.experimental import pallas as pl
from jax.experimental.pallas import tpu as pltpu
from jax.sharding import PartitionSpec as P

RESTART = 0.1
DECAY_RATE = 0.5
MESH = pl.DeviceIdType.MESH
BF = jnp.bfloat16
F32 = jnp.float32

ROWS = 1024
WIDTH = 256
FIN = 128
SLOTS = 24
DEVICES = 128
HALO = DEVICES * SLOTS
TILE = 512
GROUP = 16
VMEM_LIMIT = 64 * 2**20


def shuffled(offsets, seed):
    offsets = list(offsets)
    random.Random(seed).shuffle(offsets)
    return offsets


OFFSETS = [(k // 32, k % 4, (k // 8) % 4, (k // 4) % 2) for k in range(1, DEVICES)]
ORDER = shuffled(OFFSETS, 4)
EARLY, LATE = (1, 3), (0, 2)
ORDER_LATER = shuffled([o for o in ORDER if o[0] in EARLY], 5) + shuffled(
    [o for o in ORDER if o[0] in LATE], 6
)
PLANE = shuffled([o for o in OFFSETS if o[1] == 0 and o[3] == 0], 7)
CREW = shuffled([o for o in OFFSETS if o[0] == 0 and o[2] == 0], 8)
MIX = [math.log(DECAY_RATE / (layer + 1) + 1.0) for layer in range(2)]


def mm(a, b):
    return jnp.dot(a, b, preferred_element_type=F32)


def slope(value, sig):
    return sig * (1.0 + value * (1.0 - sig))


def kernel(
    feat_h, adj_h, halo_h, hist_h, ids_h, cnt_h, win_h, wl_h, cot_h,
    final_h, fresh_h, gsum,
    feat, adj, halo, hist, ids, cnt, win, wl, cot,
    idsend, idrecv, idcol, send, recv, pulled,
    init, x1, fin, adj_t, feat_t, wl_t, cb0_t,
    slope_in, slope0, base, ginit, gcb, gl, grad, plane_buf, crew_buf,
    in_sem, out_sem, id_send, id_recv, row_send, row_recv, sum_send, sum_recv,
):
    dom, y = lax.axis_index("dom"), lax.axis_index("rep")
    x, z, core = dom // 8, (dom // 2) % 4, dom % 2
    me = dom * 4 + y
    fwd_x = [(x + d) % 4 * 8 for d in range(4)]
    fwd_z = [(z + d) % 4 * 2 for d in range(4)]
    fwd_y = [(y + d) % 4 for d in range(4)]
    cores = [core, 1 - core]

    def ahead(off):
        return (fwd_x[off[0]] + fwd_z[off[2]] + cores[off[3]], fwd_y[off[1]])

    def behind(off):
        return (
            fwd_x[(4 - off[0]) % 4] + fwd_z[(4 - off[2]) % 4] + cores[off[3]],
            fwd_y[(4 - off[1]) % 4],
        )

    def drain(ref, sem):
        pltpu.make_async_copy(ref, ref, sem).wait()

    idrecv[pl.ds(DEVICES - 1, 1), :] = jnp.full((1, DEVICES), -1, jnp.int32)
    barrier = pltpu.get_barrier_semaphore()
    for off in ORDER:
        pl.semaphore_signal(barrier, inc=1, device_id=ahead(off), device_id_type=MESH)

    loads = [
        pltpu.make_async_copy(src, dst, in_sem.at[i])
        for i, (src, dst) in enumerate(
            [
                (ids_h, ids), (cnt_h, cnt), (hist_h, hist), (feat_h, feat), (win_h, win),
                (wl_h, wl), (adj_h, adj), (halo_h, halo), (cot_h, cot),
            ]
        )
    ]
    for load in loads:
        load.start()

    loads[0].wait()
    loads[1].wait()
    slot = lax.broadcasted_iota(jnp.int32, (SLOTS, DEVICES), 0)
    wanted = jnp.where(slot < cnt[...], ids[...], -1)
    wanted = jnp.concatenate([wanted, jnp.full((DEVICES - SLOTS, DEVICES), -1, jnp.int32)], axis=0)
    idsend[...] = wanted.T

    pl.semaphore_wait(barrier, DEVICES - 1)
    groups = [
        range(first, min(first + GROUP, DEVICES - 1)) for first in range(0, DEVICES - 1, GROUP)
    ]

    for p, off in enumerate(ORDER):
        to = behind(off)
        pltpu.make_async_remote_copy(
            src_ref=idsend.at[pl.ds(to[0] * 4 + to[1], 1)], dst_ref=idrecv.at[pl.ds(p, 1)],
            send_sem=id_send, recv_sem=id_recv, device_id=to, device_id_type=MESH,
        ).start()
    recv[0, me] = jnp.zeros((2 * SLOTS, 128), BF)
    recv[1, me] = jnp.zeros((2 * SLOTS, 128), BF)
    loads[2].wait()

    def row_copy(layer, off):
        return pltpu.make_async_remote_copy(
            src_ref=send.at[layer, ORDER.index(off)], dst_ref=recv.at[layer, me],
            send_sem=row_send.at[layer], recv_sem=row_recv.at[x if layer else 4],
            device_id=ahead(off), device_id_type=MESH,
        )

    drain(idrecv.at[pl.ds(0, DEVICES - 1)], id_recv)
    idcol[...] = idrecv[...].T
    row_id = lax.broadcasted_iota(jnp.int32, (SLOTS, ROWS), 1)
    for part in groups:
        one_hot = jnp.concatenate(
            [
                jnp.where(idcol[pl.ds(0, SLOTS), pl.ds(p, 1)] == row_id, 1.0, 0.0).astype(BF)
                for p in part
            ],
            axis=0,
        )
        for layer in range(2):
            rows = mm(one_hot, hist[layer]).astype(BF)
            for i, p in enumerate(part):
                mine = rows[i * SLOTS : (i + 1) * SLOTS]
                send[layer, p] = jnp.concatenate([mine[:, :128], mine[:, 128:]], axis=0)
            if layer == 0:
                for p in part:
                    row_copy(0, ORDER[p]).start()
    for off in ORDER_LATER:
        row_copy(1, off).start()

    for load in loads[3:7]:
        load.wait()
    for layer in range(2):
        wl_t[layer] = wl[layer].T
    feat_t[...] = feat[...].T

    @pl.loop(0, ROWS // TILE)
    def _(t):
        here = pl.ds(pl.multiple_of(t * TILE, TILE), TILE)
        pre = mm(feat[here, :], win[...])
        sig = jax.nn.sigmoid(pre)
        init[here, :] = (pre * sig).astype(BF)
        slope_in[here, :] = slope(pre, sig)
        adj_t[:, here] = adj[here, :].T

    fresh0 = pltpu.make_async_copy(init, fresh_h.at[0], out_sem.at[0])
    fresh0.start()

    def neighbours(state):
        @pl.loop(0, ROWS // TILE)
        def _(t):
            here = pl.ds(pl.multiple_of(t * TILE, TILE), TILE)
            base[here, :] = (1.0 - RESTART) * mm(adj[here, :], state[...]) + RESTART * init[
                here, :
            ].astype(F32)

    def columns_of(dx):
        return pl.ds(pl.multiple_of(fwd_x[-dx % 4] * (4 * SLOTS), 32 * SLOTS), 32 * SLOTS)

    def block(dx):
        return pl.ds(dx * 32 * SLOTS, 32 * SLOTS)

    def unpack(layer, dx):
        first = fwd_x[-dx % 4] * 4

        @pl.loop(0, 16)
        def _(o):
            both = [recv[layer, first + 2 * o], recv[layer, first + 2 * o + 1]]
            both = [jnp.concatenate([b[:SLOTS], b[SLOTS:]], axis=1) for b in both]
            rows = pl.ds(pl.multiple_of((dx * 16 + o) * 2 * SLOTS, 2 * SLOTS), 2 * SLOTS)
            pulled[rows, :] = jnp.concatenate(both, axis=0)

    def halo_sum(here, offsets):
        return functools.reduce(
            jnp.add, [mm(halo[here, columns_of(dx)], pulled[block(dx), :]) for dx in offsets]
        )

    neighbours(init)
    loads[7].wait()
    loads[8].wait()
    got = recv.at[0, pl.ds(0, DEVICES - 1)]
    pltpu.make_async_copy(got, got, row_recv.at[4]).wait()
    for dx in range(4):
        unpack(0, dx)

    @pl.loop(0, ROWS // TILE)
    def _(t):
        here = pl.ds(pl.multiple_of(t * TILE, TILE), TILE)
        comb = base[here, :] + (1.0 - RESTART) * halo_sum(here, range(4))
        comb_bf = comb.astype(BF)
        cb0_t[:, here] = comb_bf.T
        pre = (1.0 - MIX[0]) * comb + MIX[0] * mm(comb_bf, wl[0])
        sig = jax.nn.sigmoid(pre)
        x1[here, :] = (pre * sig).astype(BF)
        slope0[here, :] = slope(pre, sig)

    fresh1 = pltpu.make_async_copy(x1, fresh_h.at[1], out_sem.at[1])
    fresh1.start()
    neighbours(x1)

    def later(offsets):
        for dx in offsets:
            got = recv.at[1, pl.ds(0, 32 if dx else 31)]
            pltpu.make_async_copy(got, got, row_recv.at[(x - dx + 4) % 4]).wait()
        for dx in offsets:
            unpack(1, dx)

    later(EARLY)

    @pl.loop(0, ROWS // TILE)
    def _(t):
        here = pl.ds(pl.multiple_of(t * TILE, TILE), TILE)
        base[here, :] += (1.0 - RESTART) * halo_sum(here, EARLY)

    later(LATE)
    gl[...] = jnp.zeros_like(gl)

    @pl.loop(0, ROWS // TILE)
    def _(t):
        here = pl.ds(pl.multiple_of(t * TILE, TILE), TILE)
        comb = base[here, :] + (1.0 - RESTART) * halo_sum(here, LATE)
        comb_bf = comb.astype(BF)
        pre = (1.0 - MIX[1]) * comb + MIX[1] * mm(comb_bf, wl[1])
        sig = jax.nn.sigmoid(pre)
        fin[here, :] = (pre * sig).astype(BF)
        g_pre = cot[here, :] * slope(pre, sig)
        e = g_pre.astype(BF)
        gl[...] += mm(comb_bf.T, e)
        g_comb = (1.0 - MIX[1]) * g_pre + MIX[1] * mm(e, wl_t[1])
        ginit[here, :] = RESTART * g_comb
        gcb[0, here, :] = g_comb.astype(BF)

    final = pltpu.make_async_copy(fin, final_h, out_sem.at[2])
    final.start()

    seat, crew = x * 4 + z, y * 2 + core

    def share(part, to_x, to_z):
        if part < 2:
            row = part * WIDTH + (to_x * 4 + to_z) * 16
            return pl.ds(pl.multiple_of(row, 16), 16), pl.ds(0, WIDTH)
        row = 2 * WIDTH + (to_x * 2 + to_z // 2) * 16
        lane = to_z % 2 * 128
        return pl.ds(pl.multiple_of(row, 16), 16), pl.ds(pl.multiple_of(lane, 128), 128)

    def spread(part, stage, src, dst, off):
        return pltpu.make_async_remote_copy(
            src_ref=src, dst_ref=dst, send_sem=sum_send.at[part, stage],
            recv_sem=sum_recv.at[part, stage], device_id=ahead(off), device_id_type=MESH,
        )

    def lanes(part):
        return pl.ds(0, WIDTH if part < 2 else 128)

    def scatter(part, value):
        grad[pl.ds(part * WIDTH, value.shape[0]), :] = value.astype(BF)
        landing = plane_buf.at[part, seat, :, lanes(part)]
        for off in PLANE:
            rows, cols = share(part, fwd_x[off[0]] // 8, fwd_z[off[2]] // 2)
            spread(part, 0, grad.at[rows, cols], landing, off).start()
        rows, cols = share(part, x, z)
        plane_buf[part, seat, :, lanes(part)] = grad[rows, cols]

    def total(part, buf, stage):
        held = buf.at[part, pl.ds(0, buf.shape[1] - 1), :, lanes(part)]
        drain(held, sum_recv.at[part, stage])
        return jnp.sum(buf[part, :, :, lanes(part)].astype(F32), axis=0).astype(BF)

    def exchange(part):
        crew_buf[part, crew, :, lanes(part)] = total(part, plane_buf, 0)
        mine = crew_buf.at[part, crew, :, lanes(part)]
        for off in CREW:
            spread(part, 1, mine, mine, off).start()

    def gather(part):
        rows, cols = share(part, x, z)
        gsum[rows, cols] = total(part, crew_buf, 1)
        for off in PLANE:
            spread(part, 2, gsum.at[rows, cols], gsum.at[rows, cols], off).start()

    scatter(0, MIX[1] * gl[...])
    gl[...] = jnp.zeros_like(gl)

    @pl.loop(0, ROWS // TILE)
    def _(t):
        here = pl.ds(pl.multiple_of(t * TILE, TILE), TILE)
        g_state = (1.0 - RESTART) * mm(adj_t[here, :], gcb[0])
        g_pre = g_state * slope0[here, :]
        e = g_pre.astype(BF)
        gl[...] += mm(cb0_t[:, here], e)
        g_comb = (1.0 - MIX[0]) * g_pre + MIX[0] * mm(e, wl_t[0])
        ginit[here, :] += RESTART * g_comb
        gcb[1, here, :] = g_comb.astype(BF)

    scatter(1, MIX[0] * gl[...])
    exchange(0)
    gl[pl.ds(0, FIN), :] = jnp.zeros((FIN, WIDTH), F32)

    @pl.loop(0, ROWS // TILE)
    def _(t):
        here = pl.ds(pl.multiple_of(t * TILE, TILE), TILE)
        g_state = (1.0 - RESTART) * mm(adj_t[here, :], gcb[1])
        g_first = (ginit[here, :] + g_state) * slope_in[here, :]
        gl[pl.ds(0, FIN), :] += mm(feat_t[:, here], g_first.astype(BF))

    scatter(2, gl[pl.ds(0, FIN), :])
    exchange(1)
    gather(0)
    exchange(2)
    gather(1)
    gather(2)
    for part in range(3):
        for stage, buf in enumerate((plane_buf, crew_buf, plane_buf)):
            held = buf.at[part, pl.ds(0, buf.shape[1] - 1), :, lanes(part)]
            drain(held, sum_send.at[part, stage])
            if stage == 2:
                drain(held, sum_recv.at[part, stage])
    drain(idsend.at[pl.ds(0, DEVICES - 1)], id_send)
    drain(send.at[0, pl.ds(0, DEVICES - 1)], row_send.at[0])
    drain(send.at[1, pl.ds(0, DEVICES - 1)], row_send.at[1])
    fresh0.wait()
    fresh1.wait()
    final.wait()


def finish(
    fin, fresh, gsum, fin_out, fresh_out, grad_in, grad_layers,
    fin_held, fresh_held, gsum_held, first, layers, in_sem, out_sem,
):
    loads = [
        pltpu.make_async_copy(src, dst, in_sem.at[i])
        for i, (src, dst) in enumerate(
            [
                (gsum, gsum_held), (fin, fin_held), (fresh.at[0], fresh_held.at[0]),
                (fresh.at[1], fresh_held.at[1]),
            ]
        )
    ]
    stores = [
        pltpu.make_async_copy(src, dst, out_sem.at[i])
        for i, (src, dst) in enumerate(
            [
                (first, grad_in), (layers, grad_layers), (fin_held, fin_out),
                (fresh_held.at[0], fresh_out.at[0]), (fresh_held.at[1], fresh_out.at[1]),
            ]
        )
    ]
    for load in loads:
        load.start()
    factor = 1.0 / math.sqrt(ROWS * DEVICES)
    loads[0].wait()
    layers[0] = gsum_held[pl.ds(WIDTH, WIDTH), :].astype(F32) * factor
    layers[1] = gsum_held[pl.ds(0, WIDTH), :].astype(F32) * factor
    first[...] = gsum_held[pl.ds(2 * WIDTH, FIN), :].astype(F32) * factor
    stores[0].start()
    stores[1].start()
    for load, store in zip(loads[1:], stores[2:]):
        load.wait()
        store.start()
    for store in stores:
        store.wait()


def local(
    features, adjacency, halo_weights, history, pull_ids, pull_count, w_in, w_layers, cotangent
):
    anywhere = pl.BlockSpec(memory_space=pl.ANY)
    vmem = pltpu.VMEM
    dma = pltpu.SemaphoreType.DMA
    final_out, fresh, gsum = pl.pallas_call(
        kernel,
        out_shape=(
            jax.ShapeDtypeStruct((ROWS, WIDTH), BF),
            jax.ShapeDtypeStruct((2, ROWS, WIDTH), BF),
            jax.ShapeDtypeStruct((2 * WIDTH + FIN, WIDTH), BF),
        ),
        in_specs=[anywhere] * 9,
        out_specs=(anywhere, anywhere, pl.BlockSpec(memory_space=vmem)),
        scratch_shapes=[
            vmem((ROWS, FIN), BF),
            vmem((ROWS, ROWS), BF),
            vmem((ROWS, HALO), BF),
            vmem((2, ROWS, WIDTH), BF),
            vmem((SLOTS, DEVICES), jnp.int32),
            vmem((1, DEVICES), jnp.int32),
            vmem((FIN, WIDTH), BF),
            vmem((2, WIDTH, WIDTH), BF),
            vmem((ROWS, WIDTH), F32),
            vmem((DEVICES, 128), jnp.int32),
            vmem((DEVICES, 128), jnp.int32),
            vmem((128, DEVICES), jnp.int32),
            vmem((2, DEVICES, 2 * SLOTS, 128), BF),
            vmem((2, DEVICES, 2 * SLOTS, 128), BF),
            vmem((HALO, WIDTH), BF),
            vmem((ROWS, WIDTH), BF),
            vmem((ROWS, WIDTH), BF),
            vmem((ROWS, WIDTH), BF),
            vmem((ROWS, ROWS), BF),
            vmem((FIN, ROWS), BF),
            vmem((2, WIDTH, WIDTH), BF),
            vmem((WIDTH, ROWS), BF),
            vmem((ROWS, WIDTH), F32),
            vmem((ROWS, WIDTH), F32),
            vmem((ROWS, WIDTH), F32),
            vmem((ROWS, WIDTH), F32),
            vmem((2, ROWS, WIDTH), BF),
            vmem((WIDTH, WIDTH), F32),
            vmem((2 * WIDTH + FIN, WIDTH), BF),
            vmem((3, 16, 16, WIDTH), BF),
            vmem((3, 8, 16, WIDTH), BF),
            dma((9,)),
            dma((3,)),
            dma(()),
            dma(()),
            dma((2,)),
            dma((5,)),
            dma((3, 3)),
            dma((3, 3)),
        ],
        compiler_params=pltpu.CompilerParams(
            collective_id=0, has_side_effects=True, vmem_limit_bytes=VMEM_LIMIT
        ),
    )(
        features, adjacency, halo_weights, history, pull_ids.T, pull_count, w_in, w_layers, cotangent
    )
    return pl.pallas_call(
        finish,
        out_shape=(
            jax.ShapeDtypeStruct((ROWS, WIDTH), BF),
            jax.ShapeDtypeStruct((2, ROWS, WIDTH), BF),
            jax.ShapeDtypeStruct((FIN, WIDTH), F32),
            jax.ShapeDtypeStruct((2, WIDTH, WIDTH), F32),
        ),
        in_specs=[anywhere] * 3,
        out_specs=(anywhere,) * 4,
        scratch_shapes=[
            vmem((ROWS, WIDTH), BF),
            vmem((2, ROWS, WIDTH), BF),
            vmem((2 * WIDTH + FIN, WIDTH), BF),
            vmem((FIN, WIDTH), F32),
            vmem((2, WIDTH, WIDTH), F32),
            dma((4,)),
            dma((5,)),
        ],
        compiler_params=pltpu.CompilerParams(vmem_limit_bytes=VMEM_LIMIT),
    )(final_out, fresh, gsum)


def solution(mesh):
    rows = P(("dom", "rep"), None)
    history = P(None, ("dom", "rep"), None)
    return jax.shard_map(
        local,
        mesh=mesh,
        in_specs=(rows, rows, rows, history, rows, rows, P(), P(), rows),
        out_specs=(rows, history, P(), P()),
        check_vma=False,
    )
```

time: 94 us -> 81.5 us (0.87)
  local copies, waits for them, and re-layouts: 9 us -> 0 us
  Pallas kernels: 83.1 us -> 80.3 us
    unnamed x16 -> x0, local copies, waits for them, and re-layouts: 8.3 us -> none
    pallas_call x1, Pallas kernels: 83.1 us -> 77.9 us  [local(): pl.pallas_call(kernel, out_shape=(jax.ShapeDtypeStruct((ROWS, WIDTH), BF)...]
    pallas_call x0 -> x1, Pallas kernels: none -> 2.44 us  [local(): pl.pallas_call(finish, out_shape=(jax.ShapeDtypeStruct((ROWS, WIDTH), BF)...]
where the time goes in v2:
time: 81.5 us; the launch traced here: 81.1 us
  Pallas kernels  80.3 us (99%)
    pallas_call x1, Pallas kernels, local(): pl.pallas_call(kernel, out_shape=(jax.ShapeDtypeStruct((ROWS, WIDTH), BF)...  77.9 us
    pallas_call x1, Pallas kernels, local(): pl.pallas_call(finish, out_shape=(jax.ShapeDtypeStruct((ROWS, WIDTH), BF)...  2.44 us

profile of v2, /device:TPU:1, one launch (start us, length us, event | category | flops | bytes accessed | tf_op | source)
XLA Modules:
  0.0 81.1 jit_solution(18073393526224676476)
XLA Ops:
  0.6 77.9 %shard_map.120 = (bf16[1024,256]{1,0:T(8,128)(2,1)}, bf16[2,1024,256]{2,1,0:T(8,128)(2,1)}, bf16[640,256]{1,0:T(8,128)(2,1)}) custom-call(bf16[1024,128]{1,0:T(8,128)(2,1)} %feat_h.1, bf16[1024,1024]{1,0:T(8,128)(2,1)} %adj_h.1, bf16[1024,3072]{1,0:T(8,128)(2,1)} %halo_h.1, bf16[2,1024,256]{2,1,0:T(8,128)(2,1)} %hist_h.1, s32[24,128]{1,0:T(8,128)} %bitcast.1, ...), custom_call_target="tpu_custom_call" | custom-call | tf_op jit(solution)/shard_map/pallas_call | solution.py:390
  78.5 2.4 %shard_map.121 = (bf16[1024,256]{1,0:T(8,128)(2,1)}, bf16[2,1024,256]{2,1,0:T(8,128)(2,1)}, f32[128,256]{1,0:T(8,128)}, f32[2,256,256]{2,1,0:T(8,128)}) custom-call(bf16[1024,256]{1,0:T(8,128)(2,1)} %get-tuple-element.7.fin, bf16[2,1024,256]{2,1,0:T(8,128)(2,1)} %get-tuple-element.8.fresh, bf16[640,256]{1,0:T(8,128)(2,1)} %get-tuple-element.9.gsum), custom_call_target="tpu_custom_call" | custom-call | tf_op jit(solution)/shard_map/pallas_call | solution.py:446

commit v3 on v2

--- a/solution.py
+++ b/solution.py
@@ -21,7 +21,7 @@
 SLOTS = 24
 DEVICES = 128
 HALO = DEVICES * SLOTS
-TILE = 512
+TILE = 1024
 GROUP = 16
 VMEM_LIMIT = 64 * 2**20
 
@@ -33,11 +33,11 @@
 
 
 OFFSETS = [(k // 32, k % 4, (k // 8) % 4, (k // 4) % 2) for k in range(1, DEVICES)]
-ORDER = shuffled(OFFSETS, 4)
+ORDER = sorted(shuffled(OFFSETS, 4), key=lambda o: sum((0, 1, 2, 1)[d] for d in o[:3]))
 EARLY, LATE = (1, 3), (0, 2)
-ORDER_LATER = shuffled([o for o in ORDER if o[0] in EARLY], 5) + shuffled(
-    [o for o in ORDER if o[0] in LATE], 6
-)
+ORDER_LATER = [
+    o for half in (EARLY, LATE) for o in reversed(ORDER) if o[0] in half
+]
 PLANE = shuffled([o for o in OFFSETS if o[1] == 0 and o[3] == 0], 7)
 CREW = shuffled([o for o in OFFSETS if o[0] == 0 and o[2] == 0], 8)
 MIX = [math.log(DECAY_RATE / (layer + 1) + 1.0) for layer in range(2)]
@@ -55,7 +55,7 @@
     feat_h, adj_h, halo_h, hist_h, ids_h, cnt_h, win_h, wl_h, cot_h,
     final_h, fresh_h, gsum,
     feat, adj, halo, hist, ids, cnt, win, wl, cot,
-    idsend, idrecv, idcol, send, recv, pulled,
+    idsend, idrecv, send, recv, pulled,
     init, x1, fin, adj_t, feat_t, wl_t, cb0_t,
     slope_in, slope0, base, ginit, gcb, gl, grad, plane_buf, crew_buf,
     in_sem, out_sem, id_send, id_recv, row_send, row_recv, sum_send, sum_recv,
@@ -113,7 +113,7 @@
         to = behind(off)
         pltpu.make_async_remote_copy(
             src_ref=idsend.at[pl.ds(to[0] * 4 + to[1], 1)], dst_ref=idrecv.at[pl.ds(p, 1)],
-            send_sem=id_send, recv_sem=id_recv, device_id=to, device_id_type=MESH,
+            send_sem=id_send, recv_sem=id_recv.at[p // GROUP], device_id=to, device_id_type=MESH,
         ).start()
     recv[0, me] = jnp.zeros((2 * SLOTS, 128), BF)
     recv[1, me] = jnp.zeros((2 * SLOTS, 128), BF)
@@ -126,14 +126,14 @@
             device_id=ahead(off), device_id_type=MESH,
         )
 
-    drain(idrecv.at[pl.ds(0, DEVICES - 1)], id_recv)
-    idcol[...] = idrecv[...].T
     row_id = lax.broadcasted_iota(jnp.int32, (SLOTS, ROWS), 1)
-    for part in groups:
+    for g, part in enumerate(groups):
+        drain(idrecv.at[pl.ds(part[0], len(part))], id_recv.at[g])
+        columns = idrecv[pl.ds(g * GROUP, GROUP), :].T
         one_hot = jnp.concatenate(
             [
-                jnp.where(idcol[pl.ds(0, SLOTS), pl.ds(p, 1)] == row_id, 1.0, 0.0).astype(BF)
-                for p in part
+                jnp.where(columns[:SLOTS, i : i + 1] == row_id, 1.0, 0.0).astype(BF)
+                for i in range(len(part))
             ],
             axis=0,
         )
@@ -313,7 +313,6 @@
         gcb[1, here, :] = g_comb.astype(BF)
 
     scatter(1, MIX[0] * gl[...])
-    exchange(0)
     gl[pl.ds(0, FIN), :] = jnp.zeros((FIN, WIDTH), F32)
 
     @pl.loop(0, ROWS // TILE)
@@ -324,9 +323,10 @@
         gl[pl.ds(0, FIN), :] += mm(feat_t[:, here], g_first.astype(BF))
 
     scatter(2, gl[pl.ds(0, FIN), :])
+    exchange(0)
     exchange(1)
+    exchange(2)
     gather(0)
-    exchange(2)
     gather(1)
     gather(2)
     for part in range(3):
@@ -408,7 +408,6 @@
             vmem((ROWS, WIDTH), F32),
             vmem((DEVICES, 128), jnp.int32),
             vmem((DEVICES, 128), jnp.int32),
-            vmem((128, DEVICES), jnp.int32),
             vmem((2, DEVICES, 2 * SLOTS, 128), BF),
             vmem((2, DEVICES, 2 * SLOTS, 128), BF),
             vmem((HALO, WIDTH), BF),
@@ -431,7 +430,7 @@
             dma((9,)),
             dma((3,)),
             dma(()),
-            dma(()),
+            dma((8,)),
             dma((2,)),
             dma((5,)),
             dma((3, 3)),

time: 81.5 us -> 77.2 us (0.947)
  Pallas kernels: 80.3 us -> 76.1 us
    pallas_call x1, Pallas kernels: 77.9 us -> 73.7 us  [local(): pl.pallas_call(kernel, out_shape=(jax.ShapeDtypeStruct((ROWS, WIDTH), BF)...]
where the time goes in v3:
time: 77.2 us; the launch traced here: 76.9 us
  Pallas kernels  76.1 us (99%)
  between operations  0.8 us (1%)
    pallas_call x1, Pallas kernels, local(): pl.pallas_call(kernel, out_shape=(jax.ShapeDtypeStruct((ROWS, WIDTH), BF)...  73.7 us
    pallas_call x1, Pallas kernels, local(): pl.pallas_call(finish, out_shape=(jax.ShapeDtypeStruct((ROWS, WIDTH), BF)...  2.44 us

profile of v3, /device:TPU:1, one launch (start us, length us, event | category | flops | bytes accessed | tf_op | source)
XLA Modules:
  0.0 76.9 jit_solution(9670759070556371710)
XLA Ops:
  0.6 73.7 %shard_map.120 = (bf16[1024,256]{1,0:T(8,128)(2,1)}, bf16[2,1024,256]{2,1,0:T(8,128)(2,1)}, bf16[640,256]{1,0:T(8,128)(2,1)}) custom-call(bf16[1024,128]{1,0:T(8,128)(2,1)} %feat_h.1, bf16[1024,1024]{1,0:T(8,128)(2,1)} %adj_h.1, bf16[1024,3072]{1,0:T(8,128)(2,1)} %halo_h.1, bf16[2,1024,256]{2,1,0:T(8,128)(2,1)} %hist_h.1, s32[24,128]{1,0:T(8,128)} %bitcast.1, ...), custom_call_target="tpu_custom_call" | custom-call | tf_op jit(solution)/shard_map/pallas_call | solution.py:390
  74.3 2.4 %shard_map.121 = (bf16[1024,256]{1,0:T(8,128)(2,1)}, bf16[2,1024,256]{2,1,0:T(8,128)(2,1)}, f32[128,256]{1,0:T(8,128)}, f32[2,256,256]{2,1,0:T(8,128)}) custom-call(bf16[1024,256]{1,0:T(8,128)(2,1)} %get-tuple-element.7.fin, bf16[2,1024,256]{2,1,0:T(8,128)(2,1)} %get-tuple-element.8.fresh, bf16[640,256]{1,0:T(8,128)(2,1)} %get-tuple-element.9.gsum), custom_call_target="tpu_custom_call" | custom-call | tf_op jit(solution)/shard_map/pallas_call | solution.py:445

commit v4 on v3

--- a/solution.py
+++ b/solution.py
@@ -33,11 +33,14 @@
 
 
 OFFSETS = [(k // 32, k % 4, (k // 8) % 4, (k // 4) % 2) for k in range(1, DEVICES)]
-ORDER = sorted(shuffled(OFFSETS, 4), key=lambda o: sum((0, 1, 2, 1)[d] for d in o[:3]))
+def hops(off):
+    return sum((0, 1, 2, 1)[d] for d in off[:3])
+
+
+NEAREST = sorted(shuffled(OFFSETS, 4), key=hops)
+ORDER = NEAREST[:48] + shuffled(NEAREST[48:], 5)
 EARLY, LATE = (1, 3), (0, 2)
-ORDER_LATER = [
-    o for half in (EARLY, LATE) for o in reversed(ORDER) if o[0] in half
-]
+ORDER_LATER = [o for half in (EARLY, LATE) for o in reversed(NEAREST) if o[0] in half]
 PLANE = shuffled([o for o in OFFSETS if o[1] == 0 and o[3] == 0], 7)
 CREW = shuffled([o for o in OFFSETS if o[0] == 0 and o[2] == 0], 8)
 MIX = [math.log(DECAY_RATE / (layer + 1) + 1.0) for layer in range(2)]
@@ -55,7 +58,7 @@
     feat_h, adj_h, halo_h, hist_h, ids_h, cnt_h, win_h, wl_h, cot_h,
     final_h, fresh_h, gsum,
     feat, adj, halo, hist, ids, cnt, win, wl, cot,
-    idsend, idrecv, send, recv, pulled,
+    idsend, idrecv, one_hot, send, recv, pulled,
     init, x1, fin, adj_t, feat_t, wl_t, cb0_t,
     slope_in, slope0, base, ginit, gcb, gl, grad, plane_buf, crew_buf,
     in_sem, out_sem, id_send, id_recv, row_send, row_recv, sum_send, sum_recv,
@@ -82,7 +85,7 @@
 
     idrecv[pl.ds(DEVICES - 1, 1), :] = jnp.full((1, DEVICES), -1, jnp.int32)
     barrier = pltpu.get_barrier_semaphore()
-    for off in ORDER:
+    for off in reversed(NEAREST):
         pl.semaphore_signal(barrier, inc=1, device_id=ahead(off), device_id_type=MESH)
 
     loads = [
@@ -126,25 +129,28 @@
             device_id=ahead(off), device_id_type=MESH,
         )
 
+    def pick(layer, g, part):
+        rows = mm(one_hot[g, pl.ds(0, len(part) * SLOTS), :], hist[layer]).astype(BF)
+        for i, p in enumerate(part):
+            mine = rows[i * SLOTS : (i + 1) * SLOTS]
+            send[layer, p] = jnp.concatenate([mine[:, :128], mine[:, 128:]], axis=0)
+
     row_id = lax.broadcasted_iota(jnp.int32, (SLOTS, ROWS), 1)
     for g, part in enumerate(groups):
         drain(idrecv.at[pl.ds(part[0], len(part))], id_recv.at[g])
         columns = idrecv[pl.ds(g * GROUP, GROUP), :].T
-        one_hot = jnp.concatenate(
+        one_hot[g, pl.ds(0, len(part) * SLOTS), :] = jnp.concatenate(
             [
                 jnp.where(columns[:SLOTS, i : i + 1] == row_id, 1.0, 0.0).astype(BF)
                 for i in range(len(part))
             ],
             axis=0,
         )
-        for layer in range(2):
-            rows = mm(one_hot, hist[layer]).astype(BF)
-            for i, p in enumerate(part):
-                mine = rows[i * SLOTS : (i + 1) * SLOTS]
-                send[layer, p] = jnp.concatenate([mine[:, :128], mine[:, 128:]], axis=0)
-            if layer == 0:
-                for p in part:
-                    row_copy(0, ORDER[p]).start()
+        pick(0, g, part)
+        for p in part:
+            row_copy(0, ORDER[p]).start()
+    for g, part in enumerate(groups):
+        pick(1, g, part)
     for off in ORDER_LATER:
         row_copy(1, off).start()
 
@@ -408,6 +414,7 @@
             vmem((ROWS, WIDTH), F32),
             vmem((DEVICES, 128), jnp.int32),
             vmem((DEVICES, 128), jnp.int32),
+            vmem((DEVICES // GROUP, GROUP * SLOTS, ROWS), BF),
             vmem((2, DEVICES, 2 * SLOTS, 128), BF),
             vmem((2, DEVICES, 2 * SLOTS, 128), BF),
             vmem((HALO, WIDTH), BF),

time: 77.2 us -> 75.8 us (0.982)
  Pallas kernels: 76.1 us -> 74.9 us
    pallas_call x1, Pallas kernels: 73.7 us -> 72.4 us  [local(): pl.pallas_call(kernel, out_shape=(jax.ShapeDtypeStruct((ROWS, WIDTH), BF)...]
where the time goes in v4:
time: 75.8 us; the launch traced here: 75.7 us
  Pallas kernels  74.9 us (99%)
  between operations  0.8 us (1%)
    pallas_call x1, Pallas kernels, local(): pl.pallas_call(kernel, out_shape=(jax.ShapeDtypeStruct((ROWS, WIDTH), BF)...  72.4 us
    pallas_call x1, Pallas kernels, local(): pl.pallas_call(finish, out_shape=(jax.ShapeDtypeStruct((ROWS, WIDTH), BF)...  2.44 us

profile of v4, /device:TPU:1, one launch (start us, length us, event | category | flops | bytes accessed | tf_op | source)
XLA Modules:
  0.0 75.7 jit_solution(18040024140787873752)
XLA Ops:
  0.6 72.4 %shard_map.120 = (bf16[1024,256]{1,0:T(8,128)(2,1)}, bf16[2,1024,256]{2,1,0:T(8,128)(2,1)}, bf16[640,256]{1,0:T(8,128)(2,1)}) custom-call(bf16[1024,128]{1,0:T(8,128)(2,1)} %feat_h.1, bf16[1024,1024]{1,0:T(8,128)(2,1)} %adj_h.1, bf16[1024,3072]{1,0:T(8,128)(2,1)} %halo_h.1, bf16[2,1024,256]{2,1,0:T(8,128)(2,1)} %hist_h.1, s32[24,128]{1,0:T(8,128)} %bitcast.1, ...), custom_call_target="tpu_custom_call" | custom-call | tf_op jit(solution)/shard_map/pallas_call | solution.py:396
  73.1 2.4 %shard_map.121 = (bf16[1024,256]{1,0:T(8,128)(2,1)}, bf16[2,1024,256]{2,1,0:T(8,128)(2,1)}, f32[128,256]{1,0:T(8,128)}, f32[2,256,256]{2,1,0:T(8,128)}) custom-call(bf16[1024,256]{1,0:T(8,128)(2,1)} %get-tuple-element.7.fin, bf16[2,1024,256]{2,1,0:T(8,128)(2,1)} %get-tuple-element.8.fresh, bf16[640,256]{1,0:T(8,128)(2,1)} %get-tuple-element.9.gsum), custom_call_target="tpu_custom_call" | custom-call | tf_op jit(solution)/shard_map/pallas_call | solution.py:452

commit v5 on v4

--- a/solution.py
+++ b/solution.py
@@ -41,8 +41,8 @@
 ORDER = NEAREST[:48] + shuffled(NEAREST[48:], 5)
 EARLY, LATE = (1, 3), (0, 2)
 ORDER_LATER = [o for half in (EARLY, LATE) for o in reversed(NEAREST) if o[0] in half]
-PLANE = shuffled([o for o in OFFSETS if o[1] == 0 and o[3] == 0], 7)
-CREW = shuffled([o for o in OFFSETS if o[0] == 0 and o[2] == 0], 8)
+PLANE = [o for o in reversed(NEAREST) if o[1] == 0 and o[3] == 0]
+CREW = [o for o in reversed(NEAREST) if o[0] == 0 and o[2] == 0]
 MIX = [math.log(DECAY_RATE / (layer + 1) + 1.0) for layer in range(2)]
 
 

time: 75.8 us -> 75.1 us (level)
  no operation moved by 1% of the time
where the time goes in v5:
time: 75.1 us; the launch traced here: 75 us
  Pallas kernels  74.2 us (99%)
  between operations  0.8 us (1%)
    pallas_call x1, Pallas kernels, local(): pl.pallas_call(kernel, out_shape=(jax.ShapeDtypeStruct((ROWS, WIDTH), BF)...  71.7 us
    pallas_call x1, Pallas kernels, local(): pl.pallas_call(finish, out_shape=(jax.ShapeDtypeStruct((ROWS, WIDTH), BF)...  2.44 us

profile of v5, /device:TPU:1, one launch (start us, length us, event | category | flops | bytes accessed | tf_op | source)
XLA Modules:
  0.0 75.0 jit_solution(12245722304657968436)
XLA Ops:
  0.6 71.7 %shard_map.120 = (bf16[1024,256]{1,0:T(8,128)(2,1)}, bf16[2,1024,256]{2,1,0:T(8,128)(2,1)}, bf16[640,256]{1,0:T(8,128)(2,1)}) custom-call(bf16[1024,128]{1,0:T(8,128)(2,1)} %feat_h.1, bf16[1024,1024]{1,0:T(8,128)(2,1)} %adj_h.1, bf16[1024,3072]{1,0:T(8,128)(2,1)} %halo_h.1, bf16[2,1024,256]{2,1,0:T(8,128)(2,1)} %hist_h.1, s32[24,128]{1,0:T(8,128)} %bitcast.1, ...), custom_call_target="tpu_custom_call" | custom-call | tf_op jit(solution)/shard_map/pallas_call | solution.py:396
  72.4 2.4 %shard_map.121 = (bf16[1024,256]{1,0:T(8,128)(2,1)}, bf16[2,1024,256]{2,1,0:T(8,128)(2,1)}, f32[128,256]{1,0:T(8,128)}, f32[2,256,256]{2,1,0:T(8,128)}) custom-call(bf16[1024,256]{1,0:T(8,128)(2,1)} %get-tuple-element.7.fin, bf16[2,1024,256]{2,1,0:T(8,128)(2,1)} %get-tuple-element.8.fresh, bf16[640,256]{1,0:T(8,128)(2,1)} %get-tuple-element.9.gsum), custom_call_target="tpu_custom_call" | custom-call | tf_op jit(solution)/shard_map/pallas_call | solution.py:452
